TPU v7x, 128 devices: a whole 4x4x4 slice. The times are simulated.
128 devices in a mesh: ctx: 32 (over x, y_hi, z), tp: 4 (over y_lo, core).
Axes of the slice: x: 4, y: 4 (y_hi: 2, y_lo: 2; y = y_hi * 2 + y_lo), z: 4, core: 2. Of those that a mesh axis runs over, the one named last changes fastest.
Arguments:
- queries: bfloat16 [512, 16384], P('ctx', 'tp'), may hold values from -27 to 27
- new_keys: bfloat16 [512, 1024], P('ctx', 'tp'), may hold values from -5 to 5
- new_values: bfloat16 [512, 1024], P('ctx', 'tp'), may hold values from -5 to 5
- cache_keys: bfloat16 [65536, 1024], P('ctx', 'tp'), may hold values from -10 to 10
- cache_values: bfloat16 [65536, 1024], P('ctx', 'tp'), may hold values from -5 to 5
- cache_lens: int32 [32], P('ctx'), may hold values from 1 to 2048, 33792 in all
- out_weight: bfloat16 [16384, 16384], P('tp', 'ctx'), may hold values from -0.046875 to 0.046875
Outputs:
- attention_update: bfloat16 [512, 16384], P('tp', 'ctx')
Inputs may be any that keep to these rules, and one draw needn't show every extreme that they name: `cache_lens`: the largest entry equals 2048; the entries sum to 33792.
All inputs are finite; a program needn't handle non-finite values. No bound on the sum of `cache_lens` on one device may be relied on, other than what follows from the above.
Results may differ from a plain program's by a relative error of at most 0.02.
Values may be sent and summed in bfloat16 or wider, within the bound.
A program may use at most 576 MiB of HBM per device.

v0:
```python
import math

import jax
import jax.numpy as jnp
from jax import lax
from jax.sharding import PartitionSpec as P

HD = 128


NEG = -1e30


def body(queries, new_keys, new_values, cache_keys, cache_values, cache_lens, out_weight):
    rows = queries.shape[0]
    slots = cache_keys.shape[0]
    kv_heads = cache_keys.shape[1] // HD
    heads = queries.shape[1] // HD
    group = heads // kv_heads
    width = heads * HD
    shards = lax.axis_size("ctx")
    myself = lax.axis_index("ctx")
    length = cache_lens[0]
    scale = 1.0 / math.sqrt(HD)
    keys_old = cache_keys.reshape(slots, kv_heads, HD)
    values_old = cache_values.reshape(slots, kv_heads, HD)
    keys_new = new_keys.reshape(rows, kv_heads, HD)
    values_new = new_values.reshape(rows, kv_heads, HD)
    key_place = myself * rows + jnp.arange(rows, dtype=jnp.int32)

    def scores_of(query, keys):
        return jnp.einsum("qgrd,kgd->qgrk", query, keys, preferred_element_type=jnp.float32) * scale

    def weigh(probs, values):
        return jnp.einsum(
            "qgrk,kgd->qgrd", probs.astype(jnp.bfloat16), values, preferred_element_type=jnp.float32
        )

    def attend(block, start):
        query = block.reshape(rows, kv_heads, group, HD)
        places = start + jnp.arange(rows, dtype=jnp.int32)
        new_mask = (key_place[None, :] <= places[:, None])[:, None, None, :]
        fresh = scores_of(query, keys_new)
        old = scores_of(query, keys_old)
        old_mask = (jnp.arange(slots, dtype=jnp.int32) < length)[None, None, None, :]
        peak = jnp.maximum(
            jnp.max(jnp.where(old_mask, old, NEG), axis=-1),
            jnp.max(jnp.where(new_mask, fresh, NEG), axis=-1),
        )
        probs_old = jnp.where(old_mask, jnp.exp(old - peak[..., None]), 0.0)
        probs_new = jnp.where(new_mask, jnp.exp(fresh - peak[..., None]), 0.0)
        weight_sum = jnp.sum(probs_old, axis=-1) + jnp.sum(probs_new, axis=-1)
        summed = weigh(probs_old, values_old) + weigh(probs_new, values_new)
        partial_value = (summed / weight_sum[..., None]).astype(jnp.bfloat16)
        log_total = peak + jnp.log(weight_sum)
        return (partial_value.reshape(rows, width), log_total.reshape(rows, heads))

    piece = lax.all_gather(queries, "ctx", axis=0, tiled=True)
    count = piece.shape[0] // rows
    blocks = piece.reshape(count, rows, width)
    starts = rows * jnp.arange(count, dtype=jnp.int32)

    def one_block(pair):
        return attend(pair[0], pair[1])

    partial_value, log_total = lax.map(one_block, (blocks, starts))
    partial_value = partial_value.reshape(count * rows, width)
    log_total = log_total.reshape(count * rows, heads)
    partial_value, log_total = (partial_value, log_total)
    parts_out = lax.all_to_all(partial_value[None], "ctx", split_axis=1, concat_axis=0, tiled=True)
    parts_log = lax.all_to_all(log_total[None], "ctx", split_axis=1, concat_axis=0, tiled=True)
    top = jnp.max(parts_log, axis=0)
    weights = jnp.exp(parts_log - top[None])
    total_weight = jnp.sum(weights, axis=0)
    total_sum = jnp.sum(
        parts_out.reshape(shards, rows, heads, HD).astype(jnp.float32) * weights[..., None], axis=0
    )
    mine = total_sum / total_weight[..., None]
    heads_out = mine.reshape(rows, width).astype(jnp.bfloat16)
    terms = jnp.dot(
        lax.all_gather(heads_out, "ctx", axis=0, tiled=True),
        out_weight,
        preferred_element_type=jnp.float32,
    )
    return lax.psum_scatter(terms.astype(jnp.bfloat16), "tp", scatter_dimension=0, tiled=True)


def solution(mesh):
    in_specs = (
        P("ctx", "tp"),
        P("ctx", "tp"),
        P("ctx", "tp"),
        P("ctx", "tp"),
        P("ctx", "tp"),
        P("ctx"),
        P("tp", "ctx"),
    )
    out_specs = P("tp", "ctx")
    return jax.shard_map(body, mesh=mesh, in_specs=in_specs, out_specs=out_specs, check_vma=False)
```

profile of v0, /device:TPU:1, one launch (start us, length us, event | category | flops | bytes accessed | tf_op | source)
XLA Modules:
  0.0 600.1 jit_solution(8721989505637451881)
XLA Ops:
  7.3 1.5 copy.37
  10.8 82.9 %all-gather.3.cloned.1.call-done = bf16[512,4096]{1,0:T(8,128)(2,1)} async-done(((bf16[16,4096]{1,0:T(8,128)(2,1)}), bf16[512,4096]{1,0:T(8,128)(2,1)}) %all-gather.3.cloned.1.call-update) | async-done | bytes 4194320 | tf_op jit(solution)/shard_map/all_gather | solution.py:58
  93.7 242.3 %while.13 = (s32[]{:T(128)}, bf16[32,16,4096]{2,1,0:T(8,128)(2,1)}, f32[32,16,32]{2,1,0:T(8,128)S(1)}, s32[]{:T(128)}, bf16[32,16,4096]{2,1,0:T(8,128)(2,1)}, /*...) while((s32[]{:T(128)}, bf16[32,16,4096]{2,1,0:T(8,128)(2,1)}, ...), condition=%wide.region_5.6_spmd.clone, body=%wide.region_0.5_spmd.clone.sunk | while | flops 552871680 | bytes 17092000 | solution.py:66
  97.9 1.0 fusion.49
  105.5 1.0 fusion.49
  120.6 1.0 fusion.49
  128.2 1.0 fusion.49
  166.1 1.0 fusion.49
  196.4 1.0 fusion.49
  226.7 1.0 fusion.49
  241.8 1.0 fusion.49
  249.4 1.0 fusion.49
  257.0 1.0 fusion.49
  279.7 1.0 fusion.49
  287.2 1.0 fusion.49
  294.8 1.0 fusion.49
  302.4 1.0 fusion.49
  317.5 1.0 fusion.49
  325.1 1.0 fusion.49
  336.6 1.2 reduce.3
  338.6 5.3 all-to-all-start.1
  343.9 10.9 %copy.66 = bf16[1,512,4096]{2,0,1:T(2,128)(2,1)} copy(bf16[1,512,4096]{2,1,0:T(8,128)(2,1)} %bitcast.111) | data formatting | bytes 8388608 | tf_op jit(solution)/shard_map/broadcast_in_dim;reshape | solution.py:70
  355.4 28.4 %reduce.2 = bf16[512,4096]{1,0:T(8,128)(2,1)} reduce(bf16[512,1,4096]{2,1,0:T(2,128)(2,1)} %bitcast.107, bf16[]{:T(256)} %broadcast.61), dimensions={1}, to_apply=%bitcast.84.reduce_sub_computation | reduce | bytes 8388610
  383.8 7.8 %reshape.160 = bf16[32,2,32768]{2,1,0:T(2,128)(2,1)} reshape(bf16[512,4096]{1,0:T(8,128)(2,1)} %reduce.2) | data formatting | bytes 8388608
  391.6 9.4 %all-to-all-start = ((bf16[32,2,32768]{2,1,0:T(2,128)(2,1)}), bf16[32,2,32768]{2,1,0:T(2,128)(2,1)}, u32[]{:S(2)}, u32[]{:S(2)}) async-start(bf16[32,2,32768]{2,1,0:T(2,128)(2,1)} %reshape.160), calls=%async_computation | async-start | bytes 8388608 | tf_op jit(solution)/shard_map/all_to_all | solution.py:70
  402.5 52.7 %all-to-all-done = bf16[32,2,32768]{2,1,0:T(2,128)(2,1)} async-done(((bf16[32,2,32768]{2,1,0:T(2,128)(2,1)}), bf16[32,2,32768]{2,1,0:T(2,128)(2,1)}, u32[]{:S(2)}, u32[]{:S(2)}) %all-to-all-start) | async-done | bytes 4194336 | tf_op jit(solution)/shard_map/all_to_all | solution.py:70
  455.2 19.8 %reshape.161 = bf16[512,1,4096]{2,1,0:T(2,128)(2,1)} reshape(bf16[32,2,32768]{2,1,0:T(2,128)(2,1)} %all-to-all-done) | data formatting | bytes 8388608
  475.0 10.0 %bitcast_convert_fusion = f32[1,512,4096]{2,0,1:T(1,128)S(1)} fusion(bf16[512,1,4096]{2,1,0:T(2,128)(2,1)} %reshape.161), kind=kLoop, calls=%fused_computation.50 | loop fusion | flops 2097152 | bytes 12582912 | tf_op jit(solution)/shard_map/convert_element_type | solution.py:76
  485.0 2.5 multiply_reduce_fusion
  488.5 81.7 %all-gather.5.cloned.1.call-done = bf16[512,4096]{1,0:T(8,128)(2,1)} async-done(((bf16[16,4096]{1,0:T(8,128)(2,1)}), bf16[512,4096]{1,0:T(8,128)(2,1)}) %all-gather.5.cloned.1.call-update) | async-done | bytes 4194320 | tf_op jit(solution)/shard_map/all_gather | solution.py:81
  570.1 6.6 %convolution_convert_fusion = bf16[512,512]{1,0:T(8,128)(2,1)} fusion(bf16[512,4096]{1,0:T(8,128)(2,1)} %all-gather.5.cloned.1.call-done, bf16[4096,512]{1,0:T(8,128)(2,1)} %param.15), kind=kOutput, calls=%fused_computation.42 | convolution fusion | flops 2147745792 | bytes 8912896 | tf_op jit(solution)/shard_map/dot_general | solution.py:80
  576.7 16.8 %reduce-scatter.2.cloned.1.call-done = bf16[128,512]{1,0:T(8,128)(2,1)} async-done(((bf16[512,512]{1,0:T(8,128)(2,1)}), bf16[128,512]{1,0:T(8,128)(2,1)}) %reduce-scatter.2.cloned.1.call-update) | async-done | bytes 131088 | tf_op jit(solution)/shard_map/reduce_scatter | solution.py:85
  (655 shorter events, 230.1 us)
Async XLA Ops:
  6.5 4.3 copy-start
  6.5 2.9 copy-start.2
  6.5 87.2 %all-gather.3.cloned.1.call-start = ((), (), s32[]{:S(2)}) async-start(), calls=%async_computation.3 | async-start | bytes 4325376 | tf_op jit(solution)/shard_map/all_gather | solution.py:58
  7.3 3.5 copy-start.3
  338.6 53.0 %all-to-all-start.1 = ((f32[32,1,512]{2,1,0:T(1,128)}), f32[32,1,512]{2,1,0:T(1,128)S(1)}, u32[]{:S(2)}, u32[]{:S(2)}) async-start(f32[32,1,512]{2,1,0:T(1,128)} %reshape.162), calls=%async_computation.1 | async-start | bytes 131072 | tf_op jit(solution)/shard_map/all_to_all | solution.py:71
  391.6 63.7 %all-to-all-start = ((bf16[32,2,32768]{2,1,0:T(2,128)(2,1)}), bf16[32,2,32768]{2,1,0:T(2,128)(2,1)}, u32[]{:S(2)}, u32[]{:S(2)}) async-start(bf16[32,2,32768]{2,1,0:T(2,128)(2,1)} %reshape.160), calls=%async_computation | async-start | bytes 8388608 | tf_op jit(solution)/shard_map/all_to_all | solution.py:70
  401.0 169.2 %all-gather.5.cloned.1.call-start = ((), (), s32[]{:S(2)}) async-start(), calls=%async_computation.4 | async-start | bytes 4325376 | tf_op jit(solution)/shard_map/all_gather | solution.py:81
  488.4 105.1 %reduce-scatter.2.cloned.1.call-start = ((), (), s32[]{:S(2)}) async-start(), calls=%async_computation.5 | async-start | bytes 655360 | tf_op jit(solution)/shard_map/reduce_scatter | solution.py:85
  570.1 23.4 %copy-start.1 = (bf16[16,256]{1,0:T(8,128)(2,1)S(1)}, bf16[16,256]{1,0:T(8,128)(2,1)}, u32[]{:S(2)}) copy-start(bf16[16,256]{1,0:T(8,128)(2,1)} %param.10) | copy-start | bytes 24580
Sparse Core Ops, SparseCore 0:
  10.6 83.1 all-gather.2
  488.5 81.5 all-gather.4
  576.9 16.6 reduce-scatter.1
where the time goes:
time: 604 us; the launch traced here: 600 us
  waiting for transfers between devices  235 us (39%)
  local copies, waits for them, and re-layouts  122 us (20%)
  other arithmetic  122 us (20%)
  matrix products  90.4 us (15%)
  starting transfers between devices  14.9 us (2%)
  between operations  13.3 us (2%)
    all_gather x1, waiting for transfers between devices, body(): piece = lax.all_gather(queries, 'ctx', axis=0, tiled=True)  82.9 us
    all_gather x1, waiting for transfers between devices, body(): lax.all_gather(heads_out, 'ctx', axis=0, tiled=True)  81.7 us
    all_to_all x1, waiting for transfers between devices, body(): lax.all_to_all(partial_value[None], 'ctx', split_axis=1, concat_axis=0, t...  52.7 us
    dot_general x64, matrix products, weigh(): jnp.einsum('qgrk,kgd->qgrd', probs.astype(jnp.bfloat16), values, preferre...  43.4 us
    dot_general x64, matrix products, scores_of(): jnp.einsum('qgrd,kgd->qgrk', query, keys, preferred_element_type=jnp.floa...  40.4 us
    reduce_sum x64, other arithmetic, attend(): weight_sum = jnp.sum(probs_old, axis=-1) + jnp.sum(probs_new, axis=-1)  35.7 us
    unnamed x20, local copies, waits for them, and re-layouts  34.1 us
    while x64, local copies, waits for them, and re-layouts  30.1 us
  transfers between devices with their start and end apart: 5, of which 4 were waited for; matrix products, arithmetic and copies ran while one was open for 9% of the time, Pallas kernels for 0%

commit v1 on v0

v1 whole, which is shorter than its diff:
```python
import math

import jax
import jax.numpy as jnp
from jax import lax
from jax.experimental import pallas as pl
from jax.experimental.pallas import tpu as pltpu
from jax.sharding import PartitionSpec as P

HD = 128
NX = 4
NZ = 4
ROWS = 16
SLOTS = 2048
HEADS = 8
TOK = NX * NZ * 2 * ROWS
PIECES = 4
PIECE = HEADS // PIECES * HD
SUB = 512
NEG = -1e30
LOG2E = 1.4426950408889634
SCALE = LOG2E / math.sqrt(HD)
F32 = jnp.float32
BF16 = jnp.bfloat16
MESH = pl.DeviceIdType.MESH


def kernel(
    q_hbm, nk_hbm, nv_hbm, ck_hbm, cv_hbm, len_ref, w_hbm, out_ref,
    q, kd, vd, nkd, nvd, lens, bias, s0, s1, sn0, sn1, m0, m1, o1, mx1,
    part, lts, r1o, r1l, s2o, s2l, r2o, r2l, tmp, g, w,
    acc, es1, er1, es2, er2,
    loc, ex_s, ex_r, qa_s, qa_r, rs_s, rs_r, rl_s, rl_r, ag_s, ag_r, e_s, e_r,
):
    ctx = lax.axis_index("ctx")
    tp = lax.axis_index("tp")
    z = lax.rem(ctx, NZ)
    yh = lax.rem(ctx // NZ, 2)
    x = ctx // (2 * NZ)
    core = lax.rem(tp, 2)
    yl = tp // 2
    oh = 1 - yh

    def at(xx, hh, zz, ll, cc):
        return ((xx * 2 + hh) * NZ + zz, ll * 2 + cc)

    partner = at(x, oh, z, yl, core)
    sibling = at(x, yh, z, yl, 1 - core)
    place = ((x, z), (z, x))

    def p_peer(h, d):
        to = lax.rem(place[h][0] + d, 4)
        return to, (at(to, yh, z, yl, core) if h == 0 else at(x, yh, to, yl, core))

    def s_peer(h, d):
        to = lax.rem(place[h][1] + d, 4)
        return to, (at(x, yh, to, yl, core) if h == 0 else at(to, yh, z, yl, core))

    ends = [at(x, yh, z, 1 - yl, core), partner, at(x, oh, z, 1 - yl, core)]

    def local(src, dst, sem):
        return pltpu.make_async_copy(src, dst, sem)

    def remote(src, dst, ssem, rsem, to):
        return pltpu.make_async_remote_copy(
            src_ref=src, dst_ref=dst, send_sem=ssem, recv_sem=rsem, device_id=to, device_id_type=MESH
        )

    def await_bytes(ref, sem):
        pltpu.make_async_copy(ref, ref, sem).wait()

    def cut(start, size):
        return pl.ds(pl.multiple_of(start, size), size)

    mine = [
        local(ck_hbm.at[:, cut(yh * HD, HD)], kd.at[0, :, pl.ds(0, HD)], loc.at[0]),
        local(cv_hbm.at[:, cut(yh * HD, HD)], vd.at[0, :, pl.ds(0, HD)], loc.at[1]),
        local(nk_hbm.at[:, cut(yh * HD, HD)], nkd.at[cut(yh * ROWS, ROWS), pl.ds(0, HD)], loc.at[2]),
        local(nv_hbm.at[:, cut(yh * HD, HD)], nvd.at[cut(yh * ROWS, ROWS), pl.ds(0, HD)], loc.at[3]),
    ]
    for h in range(2):
        mine.append(
            local(
                q_hbm.at[:, cut(yh * 2048 + h * 1024, 1024)],
                q.at[h, place[h][0], place[h][1], cut(yh * ROWS, ROWS)],
                loc.at[4 + h],
            )
        )
    own_w = local(w_hbm.at[cut(yh * 2048, 2048)], w.at[yh], loc.at[6])
    for copy in mine:
        copy.start()
    own_w.start()

    lens[0] = jnp.broadcast_to(len_ref[0], (8, HD))
    nkd[32:HD, :] = jnp.zeros((HD - 32, 2 * HD), BF16)
    nvd[32:HD, :] = jnp.zeros((HD - 32, 2 * HD), BF16)

    barrier = pltpu.get_barrier_semaphore()
    greet = [partner, sibling, ends[0], ends[2]]
    for d in range(1, 4):
        greet += [p_peer(0, d)[1], s_peer(0, d)[1]]
    for to in greet:
        pl.semaphore_signal(barrier, inc=1, device_id=to, device_id_type=MESH)
    pl.semaphore_wait(barrier, len(greet))

    swaps = []
    for h in range(2):
        swaps.append(
            (
                q_hbm.at[:, cut(oh * 2048 + h * 1024, 1024)],
                q.at[h, place[h][0], place[h][1], cut(yh * ROWS, ROWS)],
            )
        )
    swaps.append((nk_hbm.at[:, cut(oh * HD, HD)], nkd.at[cut(yh * ROWS, ROWS), pl.ds(0, HD)]))
    swaps.append((nv_hbm.at[:, cut(oh * HD, HD)], nvd.at[cut(yh * ROWS, ROWS), pl.ds(0, HD)]))
    swaps.append((lens.at[0], lens.at[1]))
    swaps.append((ck_hbm.at[:, cut(oh * HD, HD)], kd.at[1, :, pl.ds(0, HD)]))
    swaps.append((cv_hbm.at[:, cut(oh * HD, HD)], vd.at[1, :, pl.ds(0, HD)]))
    swaps.append((w_hbm.at[cut(oh * 2048, 2048)], w.at[yh]))
    swap = [remote(a, b, ex_s.at[i], ex_r.at[i], partner) for i, (a, b) in enumerate(swaps)]
    for copy in swap[:7]:
        copy.start()

    mine[4].wait()
    mine[5].wait()
    swap[0].wait_recv()
    swap[1].wait_recv()

    def q_first(i):
        for h in range(2):
            ref = q.at[h, place[h][0], place[h][1], :, pl.ds(i * PIECE, PIECE)]
            for d in range(1, 4):
                remote(ref, ref, qa_s.at[0, h, i], qa_r.at[0, h, i], p_peer(h, d)[1]).start()

    def q_second(i):
        for h in range(2):
            await_bytes(q.at[h, pl.ds(0, 3), 0, :, pl.ds(i * PIECE, PIECE)], qa_r.at[0, h, i])
            ref = q.at[h, :, place[h][1], :, pl.ds(i * PIECE, PIECE)]
            for d in range(1, 4):
                remote(ref, ref, qa_s.at[1, h, i], qa_r.at[1, h, i], s_peer(h, d)[1]).start()

    def q_done(h, i):
        await_bytes(q.at[h, :, pl.ds(0, 3), :, cut(i * PIECE, PIECE)], qa_r.at[1, h, i])

    for i in range(PIECES):
        q_first(i)
    for i in range(PIECES):
        q_second(i)

    def settle(b):
        length = lens[b, 0:1, :]
        key0 = jnp.broadcast_to(kd[b, 0:1, :HD].astype(F32), (256, HD))

        def some(i, _):
            rows = cut(i * 256, 256)
            live = lax.broadcasted_iota(jnp.int32, (256, HD), 0) + i * 256 < length
            keys = jnp.where(live, kd[b, rows, :HD].astype(F32), key0).astype(BF16)
            kd[b, rows, :HD] = keys
            kd[b, rows, HD:] = keys
            vd[b, rows, :HD] = jnp.where(live, vd[b, rows, :HD].astype(F32), 0.0).astype(BF16)
            vd[b, rows, HD:] = jnp.where(live, 1.0, 0.0).astype(BF16)
            return 0

        lax.fori_loop(0, SLOTS // 256, some, 0)

    for copy in mine[:4]:
        copy.wait()
    settle(0)
    swap[2].wait_recv()
    swap[3].wait_recv()
    nkd[:32, HD:] = nkd[:32, :HD]
    nvd[:, HD:] = jnp.ones((HD, HD), BF16)
    row = lax.broadcasted_iota(jnp.int32, (TOK, HD), 0)
    lane = lax.broadcasted_iota(jnp.int32, (TOK, HD), 1)
    key_at = ((x * 2 + lane // ROWS) * NZ + z) * ROWS + lane % ROWS
    for h in range(2):
        first, second = row // 128, (row // 32) % 4
        xs, zs = (first, second) if h == 0 else (second, first)
        token = ((xs * 2 + (row // ROWS) % 2) * NZ + zs) * ROWS + row % ROWS
        bias[h] = jnp.where(jnp.logical_and(lane < 32, key_at <= token), 0.0, NEG)

    S, SN, M = (s0, s1), (sn0, sn1), (m0, m1)

    def step(b, score, weigh):
        if score is not None:
            c, h = score
            tile = q[h, :, :, :, cut(c * HD, HD)].reshape(TOK, HD).astype(F32) * SCALE
            high = tile.astype(BF16)
            low = (tile - high.astype(F32)).astype(BF16)
            query = jnp.concatenate([high, low], axis=1)
            if b == 0:
                fresh = (
                    lax.dot_general(query, nkd[...], (((1,), (1,)), ((), ())), preferred_element_type=F32)
                    + bias[h]
                )
                SN[h][...] = fresh
                peak = fresh
            else:
                peak = mx1[c, h]
        if weigh is not None:
            cw, hw = weigh
            top = M[hw][...]
            wide = jnp.tile(top, (1, SUB // HD))
            if b == 0:
                total = jnp.dot(
                    jnp.exp2(SN[hw][...] - top).astype(BF16), nvd[...], preferred_element_type=F32
                )
            else:
                fade = jnp.exp2(mx1[cw, hw] - top)
                total = o1[cw, hw] * jnp.concatenate([fade, fade], axis=1)
        for j in range(SLOTS // SUB):
            keys = slice(j * SUB, (j + 1) * SUB)
            if score is not None:
                block = lax.dot_general(
                    query, kd[b, keys, :], (((1,), (1,)), ((), ())), preferred_element_type=F32
                )
                S[h][:, keys] = block
                for t in range(SUB // HD):
                    peak = jnp.maximum(peak, block[:, t * HD : (t + 1) * HD])
            if weigh is not None:
                probs = jnp.exp2(S[hw][:, keys] - wide).astype(BF16)
                total = total + jnp.dot(probs, vd[b, keys, :], preferred_element_type=F32)
        if score is not None:
            M[h][...] = jnp.broadcast_to(jnp.max(peak, axis=1, keepdims=True), (TOK, HD))
        if weigh is None:
            return
        if b == 0:
            o1[cw, hw] = total
            mx1[cw, hw] = top
        else:
            weight = total[:, HD:]
            part[hw, cw] = (total[:, :HD] / weight).astype(BF16)
            lts[hw, cw] = (top + jnp.log(weight) * LOG2E).T[0:8, :]
            for d in range(1, 4):
                to, who = p_peer(hw, d)
                remote(
                    part.at[hw, cw, cut(to * 128, 128)], r1o.at[hw, cw, d - 1],
                    rs_s.at[0, hw, cw], rs_r.at[0, hw, cw], who,
                ).start()
                remote(
                    lts.at[hw, cw, :, cut(to * 128, 128)], r1l.at[hw, cw, d - 1],
                    rl_s.at[0, hw, cw], rl_r.at[0, hw, cw], who,
                ).start()

    def spread(line):
        return jnp.broadcast_to(line, (HD, HD)).T

    def join(parts, logs):
        top = jnp.maximum(jnp.maximum(logs[0], logs[1]), jnp.maximum(logs[2], logs[3]))
        weights = [jnp.exp2(v - top) for v in logs]
        total = weights[0] + weights[1] + weights[2] + weights[3]
        summed = weights[0] * parts[0].astype(F32)
        for i in range(1, 4):
            summed = summed + weights[i] * parts[i].astype(F32)
        return (summed / total).astype(BF16), top, total

    def serve_1(h, c):
        await_bytes(r1o.at[h, c], rs_r.at[0, h, c])
        await_bytes(r1l.at[h, c], rl_r.at[0, h, c])
        p, s = place[h]
        logs = [spread(lts[h, c, 0:1, cut(p * 128, 128)])]
        parts = [part[h, c, cut(p * 128, 128), :]]
        for i in range(3):
            logs.append(spread(r1l[h, c, i, 0:1, :]))
            parts.append(r1o[h, c, i])
        joined, top, total = join(parts, logs)
        s2o[h, c] = joined
        s2l[h, c] = (top + jnp.log(total) * LOG2E).T[0:8, :]
        for d in range(1, 4):
            to, who = s_peer(h, d)
            remote(
                s2o.at[h, c, cut(to * 32, 32)], r2o.at[h, c, d - 1],
                rs_s.at[1, h, c], rs_r.at[1, h, c], who,
            ).start()
            remote(
                s2l.at[h, c], r2l.at[h, c, d - 1], rl_s.at[1, h, c], rl_r.at[1, h, c], who
            ).start()

    def serve_2(h, c):
        await_bytes(r2o.at[h, c], rs_r.at[1, h, c])
        await_bytes(r2l.at[h, c], rl_r.at[1, h, c])
        p, s = place[h]
        tmp[0] = spread(s2l[h, c, 0:1, :])
        parts = [s2o[h, c, cut(s * 32, 32), :]]
        for i in range(3):
            tmp[i + 1] = spread(r2l[h, c, i, 0:1, :])
            parts.append(r2o[h, c, i])
        logs = [tmp[i, cut(s * 32, 32), :] for i in range(4)]
        joined, _, _ = join(parts, logs)
        g[h, p, s, :, cut(c * HD, HD)] = joined
        ref = g.at[h, p, s, :, cut(c * HD, HD)]
        for d in range(1, 4):
            remote(ref, ref, ag_s.at[0, h, c], ag_r.at[0, h, c], s_peer(h, d)[1]).start()

    def serve_3(h, c):
        p, s = place[h]
        await_bytes(g.at[h, p, pl.ds(0, 3), :, cut(c * HD, HD)], ag_r.at[0, h, c])
        ref = g.at[h, p, :, :, cut(c * HD, HD)]
        for d in range(1, 4):
            remote(ref, ref, ag_s.at[1, h, c], ag_r.at[1, h, c], p_peer(h, d)[1]).start()

    def serve_4(h, c):
        await_bytes(g.at[h, pl.ds(0, 3), :, :, cut(c * HD, HD)], ag_r.at[1, h, c])

    def serve(c, last):
        for k, act in ((1, serve_1), (2, serve_2), (3, serve_3), (4, serve_4)):
            def run(act=act, k=k):
                for h in range(2):
                    act(h, c - k)
            ok = c - k < HEADS if last else c >= k
            pl.when(ok)(run)

    for h in range(2):
        q_done(h, 0)
    step(0, (0, 0), None)

    def own(c, _):
        step(0, (c, 1), (c, 0))
        ahead = jnp.minimum(c + 1, HEADS - 1)

        @pl.when(jnp.logical_and(lax.rem(c, 2) == 1, c < HEADS - 1))
        def _():
            for h in range(2):
                q_done(h, (c + 1) // 2)

        step(0, (ahead, 0), (c, 1))
        return 0

    lax.fori_loop(0, HEADS, own, 0)

    for i in (4, 5, 6):
        swap[i].wait_recv()
    swap[7].start()
    settle(1)
    step(1, (0, 0), None)

    def other(c, _):
        step(1, (c, 1), (c, 0))
        step(1, (jnp.minimum(c + 1, HEADS - 1), 0), (c, 1))
        serve(c, False)
        return 0

    lax.fori_loop(0, HEADS, other, 0)

    def drain(c, _):
        serve(c, True)
        return 0

    lax.fori_loop(HEADS, HEADS + 4, drain, 0)

    own_w.wait()
    swap[7].wait_recv()

    def project(cc, put):
        blocks = []
        for ll in range(2):
            t = ll * 2 + cc
            blocks.append(
                jnp.concatenate(
                    [g[0, t].reshape(128, 1024), g[1, :, t].reshape(128, 1024)], axis=1
                )
            )
        heads = jnp.concatenate(blocks, axis=0)
        for k in range(2):
            res = jnp.dot(heads, w[k], preferred_element_type=F32)
            for ll in range(2):
                put(ll, k, res[ll * 128 : (ll + 1) * 128])

    def put_sent(ll, k, res):
        es1[ll, k] = res.astype(BF16)

    def put_kept(ll, k, res):
        acc[ll, k] = res

    project(1 - core, put_sent)
    to_core = remote(es1, er1, e_s.at[0], e_r.at[0], sibling)
    to_core.start()
    project(core, put_kept)
    to_core.wait_recv()
    last = []
    for i, (dl, dk) in enumerate(((1, 0), (0, 1), (1, 1))):
        ll = lax.rem(yl + dl, 2)
        k = lax.rem(yh + dk, 2)
        es2[i] = (acc[ll, k] + er1[ll, k].astype(F32)).astype(BF16)
        copy = remote(es2.at[i], er2.at[i], e_s.at[1 + i], e_r.at[1 + i], ends[i])
        copy.start()
        last.append(copy)
    result = acc[yl, yh] + er1[yl, yh].astype(F32)
    for i in range(3):
        last[i].wait_recv()
        result = result + er2[i].astype(F32)
    result = result.astype(BF16)
    for hh in range(2):
        for zz in range(NZ):
            a, b = (zz * 2 + hh) * ROWS, (hh * NZ + zz) * ROWS
            out_ref[b : b + ROWS, :] = result[a : a + ROWS]

    to_core.wait_send()
    for copy in last + swap:
        copy.wait_send()
    for h in range(2):
        for i in range(PIECES):
            cols = pl.ds(i * PIECE, PIECE)
            await_bytes(q.at[h, pl.ds(0, 3), 0, :, cols], qa_s.at[0, h, i])
            await_bytes(q.at[h, :, pl.ds(0, 3), :, cols], qa_s.at[1, h, i])

    def sent(c, _):
        cols = cut(c * HD, HD)
        for h in range(2):
            await_bytes(r1o.at[h, c], rs_s.at[0, h, c])
            await_bytes(r1l.at[h, c], rl_s.at[0, h, c])
            await_bytes(r2o.at[h, c], rs_s.at[1, h, c])
            await_bytes(r2l.at[h, c], rl_s.at[1, h, c])
            await_bytes(g.at[h, 0, pl.ds(0, 3), :, cols], ag_s.at[0, h, c])
            await_bytes(g.at[h, pl.ds(0, 3), :, :, cols], ag_s.at[1, h, c])
        return 0

    lax.fori_loop(0, HEADS, sent, 0)


def body(queries, new_keys, new_values, cache_keys, cache_values, cache_lens, out_weight):
    V = pltpu.VMEM
    D = pltpu.SemaphoreType.DMA
    any_ = pl.BlockSpec(memory_space=pl.ANY)
    return pl.pallas_call(
        kernel,
        out_shape=jax.ShapeDtypeStruct((128, 512), BF16),
        in_specs=[any_, any_, any_, any_, any_, pl.BlockSpec(memory_space=pltpu.SMEM), any_],
        out_specs=pl.BlockSpec(memory_space=pltpu.VMEM),
        scratch_shapes=[
            V((2, 4, 4, 32, 1024), BF16),
            V((2, SLOTS, 2 * HD), BF16),
            V((2, SLOTS, 2 * HD), BF16),
            V((HD, 2 * HD), BF16),
            V((HD, 2 * HD), BF16),
            V((2, 8, HD), jnp.int32),
            V((2, TOK, HD), F32),
            V((TOK, SLOTS), F32),
            V((TOK, SLOTS), F32),
            V((TOK, HD), F32),
            V((TOK, HD), F32),
            V((TOK, HD), F32),
            V((TOK, HD), F32),
            V((HEADS, 2, TOK, 2 * HD), F32),
            V((HEADS, 2, TOK, HD), F32),
            V((2, HEADS, TOK, HD), BF16),
            V((2, HEADS, 8, TOK), F32),
            V((2, HEADS, 3, 128, HD), BF16),
            V((2, HEADS, 3, 8, 128), F32),
            V((2, HEADS, 128, HD), BF16),
            V((2, HEADS, 8, 128), F32),
            V((2, HEADS, 3, 32, HD), BF16),
            V((2, HEADS, 3, 8, 128), F32),
            V((4, 128, HD), F32),
            V((2, 4, 4, 32, 1024), BF16),
            V((2, 2048, 512), BF16),
            V((2, 2, 128, 512), F32),
            V((2, 2, 128, 512), BF16),
            V((2, 2, 128, 512), BF16),
            V((3, 128, 512), BF16),
            V((3, 128, 512), BF16),
            D((7,)),
            D((8,)),
            D((8,)),
            D((2, 2, PIECES)),
            D((2, 2, PIECES)),
            D((2, 2, HEADS)),
            D((2, 2, HEADS)),
            D((2, 2, HEADS)),
            D((2, 2, HEADS)),
            D((2, 2, HEADS)),
            D((2, 2, HEADS)),
            D((4,)),
            D((4,)),
        ],
        compiler_params=pltpu.CompilerParams(
            collective_id=0, has_side_effects=True, vmem_limit_bytes=60 << 20
        ),
        cost_estimate=pl.CostEstimate(flops=20 << 30, bytes_accessed=16 << 20, transcendentals=40 << 20),
    )(queries, new_keys, new_values, cache_keys, cache_values, cache_lens, out_weight)


def solution(mesh):
    in_specs = (
        P("ctx", "tp"),
        P("ctx", "tp"),
        P("ctx", "tp"),
        P("ctx", "tp"),
        P("ctx", "tp"),
        P("ctx"),
        P("tp", "ctx"),
    )
    return jax.shard_map(body, mesh=mesh, in_specs=in_specs, out_specs=P("tp", "ctx"), check_vma=False)
```

time: 604 us -> 115 us (0.19)
  waiting for transfers between devices: 235 us -> 0 us
  other arithmetic: 122 us -> 0 us
  local copies, waits for them, and re-layouts: 122 us -> 1.57 us
  Pallas kernels: 0 us -> 113 us
  matrix products: 90.4 us -> 0 us
  starting transfers between devices: 14.9 us -> 0 us
  between operations: 13.3 us -> 0.66 us
    all_gather x2 -> x0, waiting for transfers between devices: 165 us -> none  [the longest x1 82.9 us: body(): piece = lax.all_gather(queries, 'ctx', axis=0, tiled=True)]
    pallas_call x0 -> x1, Pallas kernels: none -> 113 us  [body(): pl.pallas_call(kernel, out_shape=jax.ShapeDtypeStruct((128, 512), BF16),...]
    dot_general x129 -> x0, matrix products: 90.4 us -> none  [the longest x64 43.4 us: weigh(): jnp.einsum('qgrk,kgd->qgrd', probs.astype(jnp.bfloat16), values, preferre...]
    all_to_all x2 -> x0, waiting for transfers between devices: 52.7 us -> none  [the longest x1 52.7 us: body(): lax.all_to_all(partial_value[None], 'ctx', split_axis=1, concat_axis=0, t...]
    reduce_sum x66 -> x0, other arithmetic: 38.3 us -> none  [the longest x64 35.7 us: attend(): weight_sum = jnp.sum(probs_old, axis=-1) + jnp.sum(probs_new, axis=-1)]
    unnamed x20 -> x1, local copies, waits for them, and re-layouts: 34.1 us -> 1.57 us
    while x64 -> x0, local copies, waits for them, and re-layouts: 30.1 us -> none
    unnamed x2 -> x0, other arithmetic: 29.6 us -> none
  transfers between devices with their start and end apart: 5 -> 0, of which waited for: 4 -> 0; matrix products, arithmetic and copies ran while one was open for 9% -> 0% of each run, Pallas kernels for 0% -> 0%
where the time goes in v1:
time: 115 us
  Pallas kernels  113 us (98%)
  local copies, waits for them, and re-layouts  1.57 us (1%)
    pallas_call x1, Pallas kernels, body(): pl.pallas_call(kernel, out_shape=jax.ShapeDtypeStruct((128, 512), BF16),...  113 us

profile of v1, /device:TPU:1, one launch (start us, length us, event | category | flops | bytes accessed | tf_op | source)
XLA Modules:
  0.0 114.7 jit_solution(11961058570987115968)
XLA Ops:
  0.7 112.5 %shard_map.73 = bf16[128,512]{1,0:T(8,128)(2,1)} custom-call(bf16[16,4096]{1,0:T(8,128)(2,1)} %q_hbm.1, bf16[16,256]{1,0:T(8,128)(2,1)} %nk_hbm.1, bf16[16,256]{1,0:T(8,128)(2,1)} %nv_hbm.1, bf16[2048,256]{1,0:T(8,128)(2,1)} %ck_hbm.1, bf16[2048,256]{1,0:T(8,128)(2,1)} %cv_hbm.1, s32[1]{0:T(128)S(6)} %copy.9.len_ref, bf16[4096,512]{1,0:T(8,128)(2,1)} %w_hbm.1), custom_call_target="tpu_custom_call" | custom-call | flops 21474836480 | bytes 16777216 | tf_op jit(solution)/shard_map/pallas_call | solution.py:425
  113.2 1.6 %copy.10 = bf16[128,512]{1,0:T(8,128)(2,1)} copy(bf16[128,512]{1,0:T(8,128)(2,1)} %shard_map.73) | data formatting | bytes 262144

commit v2 on v1

v2 whole, which is shorter than its diff:
```python
import math

import jax
import jax.numpy as jnp
from jax import lax
from jax.experimental import pallas as pl
from jax.experimental.pallas import tpu as pltpu
from jax.sharding import PartitionSpec as P

HD = 128
NX = 4
NZ = 4
ROWS = 16
SLOTS = 2048
HEADS = 8
TOK = NX * NZ * 2 * ROWS
PIECES = 4
PIECE = HEADS // PIECES * HD
FIRST = ((0, PIECE), (PIECE, 1024 - PIECE), (1024, HD))
SECOND = tuple((i * PIECE, PIECE) for i in range(PIECES)) + ((1024, HD),)
LAGS = (3, 7, 11)
EARLY = 6
SUB = 512
NEG = -1e30
LOG2E = 1.4426950408889634
SCALE = LOG2E / math.sqrt(HD)
F32 = jnp.float32
BF16 = jnp.bfloat16
MESH = pl.DeviceIdType.MESH


def kernel(
    q_hbm, nk_hbm, nv_hbm, ck_hbm, cv_hbm, len_ref, w_hbm, out_ref,
    q, kd, vd, lens, s0, s1, m0, m1, oa, ob, xa, xb, ofa, ofb, mfa, mfb, fo, fl,
    part, lts, r1o, r1l, s2o, s2l, r2o, r2l, tmp, g, w,
    acc, es1, er1, es2, er2,
    loc, ex_s, ex_r, qn_s, qn_r, qf_s, qf_r, qa_s, qa_r,
    rs_s, rs_r, rl_s, rl_r, ag_s, ag_r, c_s, c_r, e_s, e_r,
):
    ctx = lax.axis_index("ctx")
    tp = lax.axis_index("tp")
    z = lax.rem(ctx, NZ)
    yh = lax.rem(ctx // NZ, 2)
    x = ctx // (2 * NZ)
    core = lax.rem(tp, 2)
    yl = tp // 2
    oh = 1 - yh

    def at(xx, hh, zz, ll, cc):
        return ((xx * 2 + hh) * NZ + zz, ll * 2 + cc)

    partner = at(x, oh, z, yl, core)
    sibling = at(x, yh, z, yl, 1 - core)
    place = ((x, z), (z, x))

    def p_peer(h, d, hh=yh):
        to = lax.rem(place[h][0] + d, 4)
        return to, (at(to, hh, z, yl, core) if h == 0 else at(x, hh, to, yl, core))

    def s_peer(h, d):
        to = lax.rem(place[h][1] + d, 4)
        return to, (at(x, yh, to, yl, core) if h == 0 else at(to, yh, z, yl, core))

    ends = [at(x, oh, z, yl, core), at(x, oh, z, 1 - yl, core), at(x, yh, z, 1 - yl, core)]

    def local(src, dst, sem):
        return pltpu.make_async_copy(src, dst, sem)

    def remote(src, dst, ssem, rsem, to):
        return pltpu.make_async_remote_copy(
            src_ref=src, dst_ref=dst, send_sem=ssem, recv_sem=rsem, device_id=to, device_id_type=MESH
        )

    def await_bytes(ref, sem):
        pltpu.make_async_copy(ref, ref, sem).wait()

    def cut(start, size):
        return pl.ds(pl.multiple_of(start, size), size)

    news = (nk_hbm, nv_hbm)
    mine = [
        local(ck_hbm.at[:, cut(yh * HD, HD)], kd.at[0, :, pl.ds(0, HD)], loc.at[0]),
        local(cv_hbm.at[:, cut(yh * HD, HD)], vd.at[0, :, pl.ds(0, HD)], loc.at[1]),
    ]
    for h in range(2):
        own_q = q.at[h, place[h][0], place[h][1], cut(yh * ROWS, ROWS)]
        mine.append(
            local(q_hbm.at[:, cut(yh * 2048 + h * 1024, 1024)], own_q.at[:, pl.ds(0, 1024)], loc.at[2 + h])
        )
        mine.append(
            local(news[h].at[:, cut(yh * HD, HD)], own_q.at[:, pl.ds(1024, HD)], loc.at[4 + h])
        )
    own_w = local(w_hbm.at[cut(yh * 2048, 2048)], w.at[yh], loc.at[6])
    for copy in mine:
        copy.start()
    own_w.start()

    barrier = pltpu.get_barrier_semaphore()
    greet = [sibling] + ends
    for d in range(1, 4):
        for h in range(2):
            greet += [p_peer(h, d)[1], p_peer(h, d, oh)[1]]
    for to in greet:
        pl.semaphore_signal(barrier, inc=1, device_id=to, device_id_type=MESH)
    lens[0] = jnp.broadcast_to(len_ref[0], (8, HD))

    fo[...] = jnp.zeros((2, HEADS, HD, HD), BF16)
    pl.semaphore_wait(barrier, len(greet))

    def q_first(i):
        start, size = FIRST[i]
        for d in (2, 1, 3, 0):
            for h in range(2):
                dst = q.at[h, place[h][0], place[h][1], cut(yh * ROWS, ROWS), pl.ds(start, size)]
                for far, hh, ss, rs in ((1, oh, qf_s, qf_r), (0, yh, qn_s, qn_r)):
                    if d == 0 and not far:
                        continue
                    if i < 2:
                        src = q_hbm.at[:, pl.ds(pl.multiple_of(hh * 2048 + h * 1024 + start, 256), size)]
                    else:
                        src = news[h].at[:, cut(hh * HD, HD)]
                    remote(src, dst, ss.at[h, i], rs.at[h, i], p_peer(h, d, hh)[1]).start()

    def q_second(i):
        start, size = SECOND[i]
        for d in (2, 1, 3):
            for h in range(2):
                ref = q.at[h, :, place[h][1], :, pl.ds(start, size)]
                remote(ref, ref, qa_s.at[h, i], qa_r.at[h, i], s_peer(h, d)[1]).start()

    def q_lines(i, sems):
        start, size = FIRST[i]
        for h in range(2):
            await_bytes(q.at[h, pl.ds(0, 3), 0, pl.ds(0, ROWS), pl.ds(start, size)], sems[0].at[h, i])
            await_bytes(q.at[h, :, 0, pl.ds(0, ROWS), pl.ds(start, size)], sems[1].at[h, i])

    def q_done(h, i):
        await_bytes(q.at[h, :, pl.ds(0, 3), :, cut(i * PIECE, PIECE)], qa_r.at[h, i])

    for i in range(3):
        q_first(i)

    swaps = (
        (lens.at[0], lens.at[1]),
        (ck_hbm.at[:, cut(oh * HD, HD)], kd.at[1, :, pl.ds(0, HD)]),
        (cv_hbm.at[:, cut(oh * HD, HD)], vd.at[1, :, pl.ds(0, HD)]),
        (w_hbm.at[cut(oh * 2048, 2048)], w.at[yh]),
    )
    swap = [remote(a, b, ex_s.at[i], ex_r.at[i], partner) for i, (a, b) in enumerate(swaps)]
    for copy in swap[:3]:
        copy.start()

    def settle(b):
        length = lens[b, 0:1, :]
        key0 = jnp.broadcast_to(kd[b, 0:1, :HD].astype(F32), (256, HD))

        def some(i, _):
            rows = cut(i * 256, 256)
            live = lax.broadcasted_iota(jnp.int32, (256, HD), 0) + i * 256 < length
            keys = jnp.where(live, kd[b, rows, :HD].astype(F32), key0).astype(BF16)
            kd[b, rows, :HD] = keys
            kd[b, rows, HD:] = keys
            vd[b, rows, :HD] = jnp.where(live, vd[b, rows, :HD].astype(F32), 0.0).astype(BF16)
            vd[b, rows, HD:] = jnp.where(live, 1.0, 0.0).astype(BF16)
            return 0

        lax.fori_loop(0, SLOTS // 256, some, 0)

    for copy in mine:
        copy.wait()
    settle(0)

    q_lines(0, (qn_r, qf_r))
    q_second(0)
    q_lines(1, (qn_r, qf_r))
    for i in range(1, PIECES):
        q_second(i)
    q_lines(2, (qn_r, qf_r))
    q_second(PIECES)

    S, M = (s0, s1), (m0, m1)
    O, MX, OF, MF = (oa, ob), (xa, xb), (ofa, ofb), (mfa, mfb)

    def split(tile):
        tile = tile.astype(F32) * SCALE
        high = tile.astype(BF16)
        low = (tile - high.astype(F32)).astype(BF16)
        return jnp.concatenate([high, low], axis=1)

    def step(score, weigh):
        if score is not None:
            c, b, h = score
            query = split(q[h, :, :, :, cut(c * HD, HD)].reshape(TOK, HD))
            peak = MX[h][c] if b else None
        if weigh is not None:
            cw, bw, hw = weigh
            top = M[hw][...]
            wide = jnp.tile(top, (1, SUB // HD))
            total = None
            if bw:
                fade = jnp.exp2(MX[hw][cw] - top)
                total = O[hw][cw] * jnp.concatenate([fade, fade], axis=1)
        for j in range(SLOTS // SUB):
            keys = slice(j * SUB, (j + 1) * SUB)
            if score is not None:
                block = lax.dot_general(
                    query, kd[b, keys, :], (((1,), (1,)), ((), ())), preferred_element_type=F32
                )
                S[h][:, keys] = block
                for t in range(SUB // HD):
                    part_of = block[:, t * HD : (t + 1) * HD]
                    peak = part_of if peak is None else jnp.maximum(peak, part_of)
            if weigh is not None:
                probs = jnp.exp2(S[hw][:, keys] - wide).astype(BF16)
                term = jnp.dot(probs, vd[bw, keys, :], preferred_element_type=F32)
                total = term if total is None else total + term
        if score is not None:
            M[h][...] = jnp.broadcast_to(jnp.max(peak, axis=1, keepdims=True), (TOK, HD))
        if weigh is not None:
            if bw:
                OF[hw][...] = total
                MF[hw][...] = top
            else:
                O[hw][cw] = total
                MX[hw][cw] = top

    def finish(h, c):
        weight = OF[h][:, HD:]
        part[h, c] = (OF[h][:, :HD] / weight).astype(BF16)
        lts[h, c] = (MF[h][...] + jnp.log(weight) * LOG2E).T[0:1, :]
        for d in (2, 1, 3):
            to, who = p_peer(h, d)
            remote(
                part.at[h, c, cut(to * 128, 128)], r1o.at[h, c, d - 1],
                rs_s.at[0, h, c], rs_r.at[0, h, c], who,
            ).start()
            remote(
                lts.at[h, c, :, cut(to * 128, 128)], r1l.at[h, c, d - 1],
                rl_s.at[0, h, c], rl_r.at[0, h, c], who,
            ).start()

    def spread(line):
        return jnp.broadcast_to(line, (HD, HD)).T

    def balance(logs):
        top = logs[0]
        for v in logs[1:]:
            top = jnp.maximum(top, v)
        weights = [jnp.exp2(v - top) for v in logs]
        total = weights[0]
        for v in weights[1:]:
            total = total + v
        return [v / total for v in weights], top + jnp.log(total) * LOG2E

    def join(parts, shares):
        summed = shares[0] * parts[0].astype(F32)
        for a, v in zip(parts[1:], shares[1:]):
            summed = summed + v * a.astype(F32)
        return summed.astype(BF16)

    def serve_1(h, c):
        await_bytes(r1o.at[h, c], rs_r.at[0, h, c])
        await_bytes(r1l.at[h, c], rl_r.at[0, h, c])
        p, s = place[h]
        shares, logs = balance(
            [lts[h, c, :, cut(p * 128, 128)]] + [r1l[h, c, i] for i in range(3)] + [fl[h, c]]
        )
        s2l[h, c] = logs
        s2o[h, c] = join(
            [part[h, c, cut(p * 128, 128), :]] + [r1o[h, c, i] for i in range(3)] + [fo[h, c]],
            [spread(v) for v in shares],
        )
        for d in (2, 1, 3):
            who = s_peer(h, d)[1]
            remote(
                s2o.at[h, c], r2o.at[h, c, d - 1], rs_s.at[1, h, c], rs_r.at[1, h, c], who
            ).start()
            remote(
                s2l.at[h, c], r2l.at[h, c, d - 1], rl_s.at[1, h, c], rl_r.at[1, h, c], who
            ).start()

    def serve_2(h, c):
        await_bytes(r2o.at[h, c], rs_r.at[1, h, c])
        await_bytes(r2l.at[h, c], rl_r.at[1, h, c])
        p, s = place[h]
        shares, _ = balance([s2l[h, c]] + [r2l[h, c, i] for i in range(3)])
        joined = join(
            [s2o[h, c]] + [r2o[h, c, i] for i in range(3)], [spread(v) for v in shares]
        )
        ref = g.at[h, p, :, :, cut(c * HD, HD)]
        g[h, p, :, :, cut(c * HD, HD)] = joined.reshape(4, 32, HD)
        for d in (2, 1, 3):
            remote(ref, ref, ag_s.at[h, c], ag_r.at[h, c], p_peer(h, d)[1]).start()

    def serve_3(h, c):
        await_bytes(g.at[h, pl.ds(0, 3), :, :, cut(c * HD, HD)], ag_r.at[h, c])

    def fresh():
        keys = q[0, :, :, :, 1024:].reshape(TOK, HD)
        keys = jnp.concatenate([keys, keys], axis=1)
        values = jnp.concatenate(
            [q[1, zz, xx, :, 1024:] for xx in range(NX) for zz in range(NZ)], axis=0
        )
        values = jnp.concatenate([values, jnp.ones((TOK, HD), BF16)], axis=1)
        rows = []
        for h in range(2):
            for c in range(HEADS):
                rows.append(q[h, place[h][0], place[h][1], :, c * HD : (c + 1) * HD])
        query = split(jnp.concatenate(rows, axis=0))
        row = lax.broadcasted_iota(jnp.int32, (TOK, TOK), 0)
        lane = lax.broadcasted_iota(jnp.int32, (TOK, TOK), 1)
        token = ((x * 2 + (row // ROWS) % 2) * NZ + z) * ROWS + row % ROWS
        key_at = ((lane // 128 * 2 + (lane // ROWS) % 2) * NZ + (lane // 32) % 4) * ROWS + lane % ROWS
        score = lax.dot_general(query, keys, (((1,), (1,)), ((), ())), preferred_element_type=F32)
        score = jnp.where(key_at <= token, score, NEG)
        top = jnp.broadcast_to(jnp.max(score, axis=1, keepdims=True), (TOK, HD))
        probs = jnp.exp2(score - jnp.tile(top, (1, TOK // HD))).astype(BF16)
        total = jnp.dot(probs, values, preferred_element_type=F32)
        weight = total[:, HD:]
        part_of = (total[:, :HD] / weight).astype(BF16).reshape(2, HEADS, 32, HD)
        logs = (top + jnp.log(weight) * LOG2E).reshape(2, HEADS, 32, HD)
        for h in range(2):
            mine_32 = cut(place[h][1] * 32, 32)
            tmp[...] = jnp.full((HD, HD), NEG, F32)
            for c in range(HEADS):
                fo[h, c, mine_32, :] = part_of[h, c]
                tmp[mine_32, :] = logs[h, c]
                fl[h, c] = tmp[...].T[0:1, :]

    def serve(c, half):
        for lag, act in ((LAGS[2], serve_3), (LAGS[1], serve_2), (LAGS[0], serve_1)):
            h = (half - lag) % 2
            j = c - (lag + h - half) // 2

            @pl.when(jnp.logical_and(j >= 0, j < HEADS))
            def _(act=act, j=j, h=h):
                act(h, j)

    for h in range(2):
        q_done(h, 0)
    step((0, 0, 0), None)

    def own(c, _):
        step((c, 0, 1), (c, 0, 0))

        @pl.when(lax.rem(c, 2) == 1)
        def _():
            for h in range(2):
                q_done(h, (c + 1) // 2)

        step((c + 1, 0, 0), (c, 0, 1))
        return 0

    LAST = HEADS - 1
    lax.fori_loop(0, LAST, own, 0)
    step((LAST, 0, 1), (LAST, 0, 0))
    for h in range(2):
        await_bytes(q.at[h, :, pl.ds(0, 3), :, pl.ds(1024, HD)], qa_r.at[h, PIECES])
    fresh()

    for copy in swap[:3]:
        copy.wait_recv()
    swap[3].start()
    settle(1)
    step((0, 1, 0), (LAST, 0, 1))
    step((0, 1, 1), (0, 1, 0))

    def other(c, _):
        finish(0, c)
        step((c + 1, 1, 0), (c, 1, 1))
        serve(c, 0)
        finish(1, c)
        step((c + 1, 1, 1), (c + 1, 1, 0))
        serve(c, 1)
        return 0

    lax.fori_loop(0, LAST, other, 0)
    finish(0, LAST)
    step(None, (LAST, 1, 1))
    finish(1, LAST)

    def drain(c, _):
        serve(c, 0)
        serve(c, 1)
        return 0

    BREAK = (2 * HEADS - 1 + LAGS[1]) // 2 + 1
    lax.fori_loop(LAST, BREAK, drain, 0)

    def heads_of(cc, first, count):
        blocks = []
        cols = pl.ds(first * HD, count * HD)
        for ll in range(2):
            t = ll * 2 + cc
            blocks.append(
                jnp.concatenate(
                    [
                        g[0, t, :, :, cols].reshape(128, count * HD),
                        g[1, :, t, :, cols].reshape(128, count * HD),
                    ],
                    axis=1,
                )
            )
        return jnp.concatenate(blocks, axis=0)

    def project(heads, k, first, count):
        size = count * HD
        top = jnp.dot(heads[:, :size], w[k, pl.ds(first * HD, size)], preferred_element_type=F32)
        return top + jnp.dot(
            heads[:, size:], w[k, pl.ds(1024 + first * HD, size)], preferred_element_type=F32
        )

    own_w.wait()
    for k in (yh, oh):
        if k is oh:
            swap[3].wait_recv()
        for a, cc in enumerate((1 - core, core)):
            acc[a, k] = project(heads_of(cc, 0, EARLY), k, 0, EARLY)

    lax.fori_loop(BREAK, (2 * HEADS - 1 + LAGS[2]) // 2 + 1, drain, 0)

    to_core = []
    late = HEADS - EARLY
    for k in (oh, yh):
        es1[k] = (acc[0, k] + project(heads_of(1 - core, EARLY, late), k, EARLY, late)).astype(BF16)
        copy = remote(es1.at[k], er1.at[k], c_s.at[k], c_r.at[k], sibling)
        copy.start()
        to_core.append(copy)
    for k in (oh, yh):
        acc[1, k] += project(heads_of(core, EARLY, late), k, EARLY, late)
    last = []

    def send(i, ll, k):
        rows = cut(ll * 128, 128)
        es2[i] = (acc[1, k, rows, :] + er1[k, rows, :].astype(F32)).astype(BF16)
        copy = remote(es2.at[i], er2.at[i], e_s.at[i], e_r.at[i], ends[i])
        copy.start()
        last.append(copy)

    to_core[0].wait_recv()
    send(0, yl, oh)
    send(1, 1 - yl, oh)
    to_core[1].wait_recv()
    send(2, 1 - yl, yh)
    rows = cut(yl * 128, 128)
    result = acc[1, yh, rows, :] + er1[yh, rows, :].astype(F32)
    for i in (2, 1, 0):
        last[i].wait_recv()
        result = result + er2[i].astype(F32)
    result = result.astype(BF16)
    for hh in range(2):
        for zz in range(NZ):
            a, b = (zz * 2 + hh) * ROWS, (hh * NZ + zz) * ROWS
            out_ref[b : b + ROWS, :] = result[a : a + ROWS]

    for copy in to_core + last + swap:
        copy.wait_send()
    for i in range(3):
        q_lines(i, (qn_s, qf_s))
    for h in range(2):
        for i in range(PIECES + 1):
            start, size = SECOND[i]
            await_bytes(q.at[h, :, pl.ds(0, 3), :, pl.ds(start, size)], qa_s.at[h, i])

    def sent(c, _):
        cols = cut(c * HD, HD)
        for h in range(2):
            await_bytes(r1o.at[h, c], rs_s.at[0, h, c])
            await_bytes(r1l.at[h, c], rl_s.at[0, h, c])
            await_bytes(r2o.at[h, c], rs_s.at[1, h, c])
            await_bytes(r2l.at[h, c], rl_s.at[1, h, c])
            await_bytes(g.at[h, pl.ds(0, 3), :, :, cols], ag_s.at[h, c])
        return 0

    lax.fori_loop(0, HEADS, sent, 0)


def body(queries, new_keys, new_values, cache_keys, cache_values, cache_lens, out_weight):
    V = pltpu.VMEM
    D = pltpu.SemaphoreType.DMA
    any_ = pl.BlockSpec(memory_space=pl.ANY)
    return pl.pallas_call(
        kernel,
        out_shape=jax.ShapeDtypeStruct((128, 512), BF16),
        in_specs=[any_, any_, any_, any_, any_, pl.BlockSpec(memory_space=pltpu.SMEM), any_],
        out_specs=pl.BlockSpec(memory_space=pltpu.VMEM),
        scratch_shapes=[
            V((2, 4, 4, 32, 1152), BF16),
            V((2, SLOTS, 2 * HD), BF16),
            V((2, SLOTS, 2 * HD), BF16),
            V((2, 8, HD), jnp.int32),
            V((TOK, SLOTS), F32),
            V((TOK, SLOTS), F32),
            V((TOK, HD), F32),
            V((TOK, HD), F32),
            V((HEADS, TOK, 2 * HD), F32),
            V((HEADS, TOK, 2 * HD), F32),
            V((HEADS, TOK, HD), F32),
            V((HEADS, TOK, HD), F32),
            V((TOK, 2 * HD), F32),
            V((TOK, 2 * HD), F32),
            V((TOK, HD), F32),
            V((TOK, HD), F32),
            V((2, HEADS, HD, HD), BF16),
            V((2, HEADS, 1, HD), F32),
            V((2, HEADS, TOK, HD), BF16),
            V((2, HEADS, 1, TOK), F32),
            V((2, HEADS, 3, 128, HD), BF16),
            V((2, HEADS, 3, 1, 128), F32),
            V((2, HEADS, 128, HD), BF16),
            V((2, HEADS, 1, 128), F32),
            V((2, HEADS, 3, 128, HD), BF16),
            V((2, HEADS, 3, 1, 128), F32),
            V((HD, HD), F32),
            V((2, 4, 4, 32, 1024), BF16),
            V((2, 2048, 512), BF16),
            V((2, 2, 256, 512), F32),
            V((2, 256, 512), BF16),
            V((2, 256, 512), BF16),
            V((3, 128, 512), BF16),
            V((3, 128, 512), BF16),
            D((7,)),
            D((4,)),
            D((4,)),
            D((2, 3)),
            D((2, 3)),
            D((2, 3)),
            D((2, 3)),
            D((2, PIECES + 1)),
            D((2, PIECES + 1)),
            D((2, 2, HEADS)),
            D((2, 2, HEADS)),
            D((2, 2, HEADS)),
            D((2, 2, HEADS)),
            D((2, HEADS)),
            D((2, HEADS)),
            D((2,)),
            D((2,)),
            D((3,)),
            D((3,)),
        ],
        compiler_params=pltpu.CompilerParams(
            collective_id=0, has_side_effects=True, vmem_limit_bytes=60 << 20
        ),
        cost_estimate=pl.CostEstimate(flops=20 << 30, bytes_accessed=16 << 20, transcendentals=40 << 20),
    )(queries, new_keys, new_values, cache_keys, cache_values, cache_lens, out_weight)


def solution(mesh):
    in_specs = (
        P("ctx", "tp"),
        P("ctx", "tp"),
        P("ctx", "tp"),
        P("ctx", "tp"),
        P("ctx", "tp"),
        P("ctx"),
        P("tp", "ctx"),
    )
    return jax.shard_map(body, mesh=mesh, in_specs=in_specs, out_specs=P("tp", "ctx"), check_vma=False)
```

time: 115 us -> 106 us (0.922)
  Pallas kernels: 113 us -> 103 us
    pallas_call x1, Pallas kernels: 113 us -> 103 us  [body(): pl.pallas_call(kernel, out_shape=jax.ShapeDtypeStruct((128, 512), BF16),...]
where the time goes in v2:
time: 106 us
  Pallas kernels  103 us (97%)
  local copies, waits for them, and re-layouts  1.57 us (1%)
    pallas_call x1, Pallas kernels, body(): pl.pallas_call(kernel, out_shape=jax.ShapeDtypeStruct((128, 512), BF16),...  103 us

profile of v2, /device:TPU:1, one launch (start us, length us, event | category | flops | bytes accessed | tf_op | source)
XLA Modules:
  0.0 105.7 jit_solution(8038418650797049828)
XLA Ops:
  0.7 103.5 %shard_map.73 = bf16[128,512]{1,0:T(8,128)(2,1)} custom-call(bf16[16,4096]{1,0:T(8,128)(2,1)} %q_hbm.1, bf16[16,256]{1,0:T(8,128)(2,1)} %nk_hbm.1, bf16[16,256]{1,0:T(8,128)(2,1)} %nv_hbm.1, bf16[2048,256]{1,0:T(8,128)(2,1)} %ck_hbm.1, bf16[2048,256]{1,0:T(8,128)(2,1)} %cv_hbm.1, s32[1]{0:T(128)S(6)} %copy.9.len_ref, bf16[4096,512]{1,0:T(8,128)(2,1)} %w_hbm.1), custom_call_target="tpu_custom_call" | custom-call | flops 21474836480 | bytes 16777216 | tf_op jit(solution)/shard_map/pallas_call | solution.py:482
  104.1 1.6 %copy.10 = bf16[128,512]{1,0:T(8,128)(2,1)} copy(bf16[128,512]{1,0:T(8,128)(2,1)} %shard_map.73) | data formatting | bytes 262144

commit v3 on v2

--- a/solution.py
+++ b/solution.py
@@ -14,11 +14,11 @@
 SLOTS = 2048
 HEADS = 8
 TOK = NX * NZ * 2 * ROWS
-PIECES = 4
+PIECES = 8
 PIECE = HEADS // PIECES * HD
 FIRST = ((0, PIECE), (PIECE, 1024 - PIECE), (1024, HD))
 SECOND = tuple((i * PIECE, PIECE) for i in range(PIECES)) + ((1024, HD),)
-LAGS = (3, 7, 11)
+LAGS = (3, 7, 12)
 EARLY = 6
 SUB = 512
 NEG = -1e30
@@ -116,7 +116,7 @@
                     if d == 0 and not far:
                         continue
                     if i < 2:
-                        src = q_hbm.at[:, pl.ds(pl.multiple_of(hh * 2048 + h * 1024 + start, 256), size)]
+                        src = q_hbm.at[:, pl.ds(pl.multiple_of(hh * 2048 + h * 1024 + start, HD), size)]
                     else:
                         src = news[h].at[:, cut(hh * HD, HD)]
                     remote(src, dst, ss.at[h, i], rs.at[h, i], p_peer(h, d, hh)[1]).start()
@@ -147,9 +147,6 @@
         (w_hbm.at[cut(oh * 2048, 2048)], w.at[yh]),
     )
     swap = [remote(a, b, ex_s.at[i], ex_r.at[i], partner) for i, (a, b) in enumerate(swaps)]
-    for copy in swap[:3]:
-        copy.start()
-
     def settle(b):
         length = lens[b, 0:1, :]
         key0 = jnp.broadcast_to(kd[b, 0:1, :HD].astype(F32), (256, HD))
@@ -175,8 +172,8 @@
     q_lines(1, (qn_r, qf_r))
     for i in range(1, PIECES):
         q_second(i)
-    q_lines(2, (qn_r, qf_r))
-    q_second(PIECES)
+    for copy in swap[:3]:
+        copy.start()
 
     S, M = (s0, s1), (m0, m1)
     O, MX, OF, MF = (oa, ob), (xa, xb), (ofa, ofb), (mfa, mfb)
@@ -343,10 +340,13 @@
     def own(c, _):
         step((c, 0, 1), (c, 0, 0))
 
-        @pl.when(lax.rem(c, 2) == 1)
+        @pl.when(c == 1)
         def _():
-            for h in range(2):
-                q_done(h, (c + 1) // 2)
+            q_lines(2, (qn_r, qf_r))
+            q_second(PIECES)
+
+        for h in range(2):
+            q_done(h, c + 1)
 
         step((c + 1, 0, 0), (c, 0, 1))
         return 0
@@ -426,8 +426,6 @@
         copy = remote(es1.at[k], er1.at[k], c_s.at[k], c_r.at[k], sibling)
         copy.start()
         to_core.append(copy)
-    for k in (oh, yh):
-        acc[1, k] += project(heads_of(core, EARLY, late), k, EARLY, late)
     last = []
 
     def send(i, ll, k):
@@ -437,9 +435,11 @@
         copy.start()
         last.append(copy)
 
+    acc[1, oh] += project(heads_of(core, EARLY, late), oh, EARLY, late)
     to_core[0].wait_recv()
     send(0, yl, oh)
     send(1, 1 - yl, oh)
+    acc[1, yh] += project(heads_of(core, EARLY, late), yh, EARLY, late)
     to_core[1].wait_recv()
     send(2, 1 - yl, yh)
     rows = cut(yl * 128, 128)

time: 106 us -> 105 us (level)
  no operation moved by 1% of the time
where the time goes in v3:
time: 105 us
  Pallas kernels  103 us (98%)
  local copies, waits for them, and re-layouts  1.57 us (1%)
    pallas_call x1, Pallas kernels, body(): pl.pallas_call(kernel, out_shape=jax.ShapeDtypeStruct((128, 512), BF16),...  103 us

profile of v3, /device:TPU:1, one launch (start us, length us, event | category | flops | bytes accessed | tf_op | source)
XLA Modules:
  0.0 105.2 jit_solution(14620086839362871470)
XLA Ops:
  0.7 103.0 %shard_map.73 = bf16[128,512]{1,0:T(8,128)(2,1)} custom-call(bf16[16,4096]{1,0:T(8,128)(2,1)} %q_hbm.1, bf16[16,256]{1,0:T(8,128)(2,1)} %nk_hbm.1, bf16[16,256]{1,0:T(8,128)(2,1)} %nv_hbm.1, bf16[2048,256]{1,0:T(8,128)(2,1)} %ck_hbm.1, bf16[2048,256]{1,0:T(8,128)(2,1)} %cv_hbm.1, s32[1]{0:T(128)S(6)} %copy.9.len_ref, bf16[4096,512]{1,0:T(8,128)(2,1)} %w_hbm.1), custom_call_target="tpu_custom_call" | custom-call | flops 21474836480 | bytes 16777216 | tf_op jit(solution)/shard_map/pallas_call | solution.py:482
  103.7 1.6 %copy.10 = bf16[128,512]{1,0:T(8,128)(2,1)} copy(bf16[128,512]{1,0:T(8,128)(2,1)} %shard_map.73) | data formatting | bytes 262144
